TPU v7x, 512 devices: a whole 4x8x8 slice. The times are simulated.
512 devices in a mesh: sub: 16 (over z, core), region: 32 (over y, x).
Axes of the slice: x: 4, y: 8, z: 8, core: 2. Of those that a mesh axis runs over, the one named last changes fastest.
Arguments:
- residual: bfloat16 [16, 32, 512, 1024], P('sub', 'region'), may hold values from -6 to 6
- send_rows: int32 [16, 32, 4, 64], P('sub', 'region'), may hold values from 0 to 511
- local_inverse: bfloat16 [16, 32, 512, 768], P('sub', 'region'), may hold values from -0.21875 to 0.21875
- coarse_basis: bfloat16 [16, 32, 512, 128], P('sub', 'region'), may hold values from -0.25 to 0.25
- regional_inverse: bfloat16 [16, 32, 128, 2048], P('sub', 'region'), may hold values from -0.125 to 0.125
- root_map: bfloat16 [16, 32, 128, 64], P('sub', 'region'), may hold values from -0.75 to 0.75
- root_inverse: bfloat16 [32, 64, 2048], P('region'), may hold values from -0.0234375 to 0.0234375
Outputs:
- correction: bfloat16 [16, 32, 512, 1024], P('sub', 'region')
All inputs are finite; a program needn't handle non-finite values.
Results may differ from a plain program's by a relative error of at most 0.0055.
Values may be sent and summed in bfloat16 or wider, within the bound.
A program may use at most 64 MiB of HBM per device.

v0:
```python
import jax
import jax.numpy as jnp
from jax import lax
from jax.sharding import PartitionSpec as P


def extended(shard, sides, width):
    for axis, dim in sides:
        devices, length = (lax.axis_size(axis), shard.shape[dim])
        up = [(i, (i + 1) % devices) for i in range(devices - 1)]
        down = [(j, i) for i, j in up]
        last = lax.slice_in_dim(shard, length - width, length, axis=dim)
        leading = lax.slice_in_dim(shard, 0, width, axis=dim)
        before = lax.ppermute(last, axis, up)
        after = lax.ppermute(leading, axis, down)
        shard = jnp.concatenate([before, shard, after], axis=dim)
    return shard


def split_up(shard, dim, devices):
    before, after = (shard.shape[:dim], shard.shape[dim + 1 :])
    return jnp.moveaxis(shard.reshape(*before, devices, -1, *after), dim, 0)


def summed_on_arrival(shard, axis, dim):
    blocks = split_up(shard, dim, lax.axis_size(axis))
    arrived = lax.all_to_all(blocks, axis, split_axis=0, concat_axis=0, tiled=True)
    return arrived.sum(axis=0)


def laid_out(blocks, dim):
    dims = list(blocks.shape[1:])
    dims[dim] *= blocks.shape[0]
    return jnp.moveaxis(blocks, 0, dim).reshape(dims)


def sent_to_all(shard, axis):
    devices = lax.axis_size(axis)
    return lax.all_to_all(
        jnp.broadcast_to(shard[None], (devices, *shard.shape)), axis, 0, 0, tiled=True
    )


def gather_directly(shard, axis, dim):
    return laid_out(sent_to_all(shard, axis), dim)


def regional_solve(coarse_rhs, regional_rows):
    return jnp.dot(
        regional_rows,
        lax.all_gather(coarse_rhs, "sub", axis=0, tiled=True),
        preferred_element_type=jnp.float32,
    )


def project_root(root_part, coarse_rhs):
    return lax.dot_general(
        root_part, coarse_rhs, (((0,), (0,)), ((), ())), preferred_element_type=jnp.float32
    )


def per_device(
    residual, send_rows, local_inverse, coarse_basis, regional_inverse, root_map, root_inverse
):
    owned = residual[0, 0]
    rows_lent = send_rows[0, 0]
    margin = rows_lent.shape[1]
    columns = owned.shape[1]
    lent = jnp.take(owned, rows_lent.reshape(-1), axis=0).reshape(4, margin, columns)
    sub_ext = extended(lent[:2].reshape(2 * margin, columns), (("sub", 0),), margin)
    reg_ext = extended(lent[2:].reshape(2 * margin, columns), (("region", 0),), margin)
    sub_vec = jnp.concatenate(
        [owned, sub_ext[:margin], sub_ext[-margin:], reg_ext[:margin], reg_ext[-margin:]], axis=0
    )
    local = jnp.dot(local_inverse[0, 0], sub_vec, preferred_element_type=jnp.float32)
    basis = coarse_basis[0, 0]
    coarse_rhs = lax.dot_general(
        basis, owned, (((0,), (0,)), ((), ())), preferred_element_type=jnp.float32
    ).astype(jnp.bfloat16)
    regional_rows = regional_inverse[0, 0]
    root_part = root_map[0, 0]
    root_rows = root_inverse[0]
    regional = regional_solve(coarse_rhs, regional_rows)
    block_rhs = summed_on_arrival(project_root(root_part, coarse_rhs), "sub", 1).astype(
        jnp.bfloat16
    )
    block_sol = jnp.dot(
        root_rows, gather_directly(block_rhs, "region", 0), preferred_element_type=jnp.float32
    ).astype(jnp.bfloat16)
    root_sol = gather_directly(block_sol, "sub", 1)
    weights = (regional + jnp.dot(root_part, root_sol, preferred_element_type=jnp.float32)).astype(
        jnp.bfloat16
    )
    total = local + jnp.dot(basis, weights, preferred_element_type=jnp.float32)
    return total.astype(jnp.bfloat16).reshape(1, 1, owned.shape[0], columns)


def solution(mesh):
    in_specs = (
        P("sub", "region", None, None),
        P("sub", "region", None, None),
        P("sub", "region", None, None),
        P("sub", "region", None, None),
        P("sub", "region", None, None),
        P("sub", "region", None, None),
        P("region", None, None),
    )
    out_specs = P("sub", "region", None, None)
    return jax.shard_map(
        per_device, mesh=mesh, in_specs=in_specs, out_specs=out_specs, check_vma=False
    )
```

profile of v0, /device:TPU:33, one launch (start us, length us, event | category | flops | bytes accessed | tf_op | source)
XLA Modules:
  0.0 96.9 jit_solution(17243275777025831644)
XLA Ops:
  6.5 2.4 %convolution_convert_fusion = bf16[128,1024]{1,0:T(8,128)(2,1)} fusion(bf16[1,1,512,128]{3,2,1,0:T(8,128)(2,1)} %param.10, bf16[1,1,512,1024]{3,2,1,0:T(8,128)(2,1)} %param.7), kind=kOutput, calls=%fused_computation.4 | convolution fusion | flops 134348800 | bytes 1441792 | tf_op jit(solution)/shard_map/dot_general | solution.py:77
  9.0 1.1 %convolution_bitcast_fusion = f32[64,1024]{1,0:T(8,128)S(1)} fusion(bf16[128,1024]{1,0:T(8,128)(2,1)} %convolution_convert_fusion, bf16[1,1,128,64]{2,3,1,0:T(8,128)(2,1)S(1)} %copy-done.4), kind=kOutput, calls=%fused_computation.6 | convolution fusion | flops 16777216 | bytes 540672 | tf_op jit(solution)/shard_map/dot_general | solution.py:57
  10.5 1.0 %reshape.71 = f32[16,1,4096]{2,1,0:T(1,128)} reshape(f32[16,64,64]{2,1,0:T(8,128)S(1)} %bitcast.44) | data formatting | bytes 524288
  11.5 11.0 %all-to-all-start = ((f32[16,1,4096]{2,1,0:T(1,128)}), f32[16,1,4096]{2,1,0:T(1,128)S(1)}, u32[]{:S(2)}, u32[]{:S(2)}) async-start(f32[16,1,4096]{2,1,0:T(1,128)} %reshape.71), calls=%async_computation | async-start | bytes 524288 | tf_op jit(solution)/shard_map/all_to_all | solution.py:27
  22.7 1.2 %gather_fusion = bf16[256,1024]{1,0:T(8,128)(2,1)S(1)} fusion(bf16[512,1024]{1,0:T(8,128)(2,1)S(1)} %bitcast.43, s32[1024]{0:T(1024)S(1)} %pad_clamp_fusion), kind=kCustom, calls=%fused_computation | custom fusion | bytes 1049600 | tf_op jit(solution)/shard_map/jit(_take)/gather | solution.py:69
  24.0 10.2 %all-to-all-done = f32[16,1,4096]{2,1,0:T(1,128)S(1)} async-done(((f32[16,1,4096]{2,1,0:T(1,128)}), f32[16,1,4096]{2,1,0:T(1,128)S(1)}, u32[]{:S(2)}, u32[]{:S(2)}) %all-to-all-start) | async-done | bytes 262176 | tf_op jit(solution)/shard_map/all_to_all | solution.py:27
  34.7 1.2 %reduce = f32[16,4096]{1,0:T(8,128)S(1)} reduce(f32[16,1,4096]{2,1,0:T(1,128)S(1)} %all-to-all-done, f32[]{:T(128)} %broadcast.30), dimensions={1}, to_apply=%all_to_all.9.reduce_sub_computation | reduce | bytes 524292 | tf_op jit(solution)/shard_map/all_to_all | solution.py:27
  36.2 1.1 %reshape.73 = bf16[32,2,2048]{2,1,0:T(2,128)(2,1)} reshape(bf16[32,64,64]{2,1,0:T(8,128)(2,1)S(1)} %broadcast_in_dim.24) | data formatting | bytes 524288
  37.3 9.3 %all-to-all-start.1 = ((bf16[32,2,2048]{2,1,0:T(2,128)(2,1)}), bf16[32,2,2048]{2,1,0:T(2,128)(2,1)S(1)}, u32[]{:S(2)}, u32[]{:S(2)}) async-start(bf16[32,2,2048]{2,1,0:T(2,128)(2,1)} %reshape.73), calls=%async_computation.1 | async-start | bytes 524288 | tf_op jit(solution)/shard_map/all_to_all | solution.py:39
  46.6 2.1 %collective-permute-start = (bf16[64,1024]{1,0:T(8,128)(2,1)S(1)}, bf16[64,1024]{1,0:T(8,128)(2,1)S(1)}, u32[]{:S(2)}, u32[]{:S(2)}) collective-permute-start(bf16[64,1024]{1,0:T(8,128)(2,1)S(1)} %get-tuple-element.8), channel_id=1, source_target_pairs={{0,32},{32,64},{64,96},{96,128},{128,160},{160,192},{192,224},{224... | collective-permute-start | bytes 393224 | tf_op jit(solution)/shard_map/ppermute | solution.py:14
  48.7 2.3 %collective-permute-start.1 = (bf16[64,1024]{1,0:T(8,128)(2,1)S(1)}, bf16[64,1024]{1,0:T(8,128)(2,1)S(1)}, u32[]{:S(2)}, u32[]{:S(2)}) collective-permute-start(bf16[64,1024]{1,0:T(8,128)(2,1)S(1)} %get-tuple-element.7), channel_id=1, source_target_pairs={{32,0},{64,32},{96,64},{128,96},{160,128},{192,160},{224,192},{256... | collective-permute-start | bytes 393224 | tf_op jit(solution)/shard_map/ppermute | solution.py:15
  51.0 3.1 %collective-permute-start.2 = (bf16[64,1024]{1,0:T(8,128)(2,1)S(1)}, bf16[64,1024]{1,0:T(8,128)(2,1)S(1)}, u32[]{:S(2)}, u32[]{:S(2)}) collective-permute-start(bf16[64,1024]{1,0:T(8,128)(2,1)S(1)} %get-tuple-element.6), channel_id=1, source_target_pairs={{0,1},{1,2},{2,3},{3,4},{4,5},{5,6},{6,7},{7,8},{8,9},{9,10},{10,1... | collective-permute-start | bytes 393224 | tf_op jit(solution)/shard_map/ppermute | solution.py:14
  54.1 5.6 %collective-permute-start.3 = (bf16[64,1024]{1,0:T(8,128)(2,1)S(1)}, bf16[64,1024]{1,0:T(8,128)(2,1)S(1)}, u32[]{:S(2)}, u32[]{:S(2)}) collective-permute-start(bf16[64,1024]{1,0:T(8,128)(2,1)S(1)} %get-tuple-element.5), channel_id=1, source_target_pairs={{1,0},{2,1},{3,2},{4,3},{5,4},{6,5},{7,6},{8,7},{9,8},{10,9},{11,1... | collective-permute-start | bytes 393224 | tf_op jit(solution)/shard_map/ppermute | solution.py:15
  59.8 1.0 %constant_dynamic-update-slice_fusion.4 = bf16[768,1024]{1,0:T(8,128)(2,1)} fusion(bf16[1,1,512,1024]{3,2,1,0:T(8,128)(2,1)S(1)} %copy-done.1), kind=kLoop, calls=%fused_computation.24 | loop fusion | bytes 2097152
  60.8 0.7 constant_dynamic-update-slice_fusion.3
  62.3 0.9 reshape.75
  63.2 7.1 %all-to-all-start.2 = ((bf16[16,2,2048]{2,1,0:T(2,128)(2,1)}), bf16[16,2,2048]{2,1,0:T(2,128)(2,1)S(1)}, u32[]{:S(2)}, u32[]{:S(2)}) async-start(bf16[16,2,2048]{2,1,0:T(2,128)(2,1)} %reshape.75), calls=%async_computation.2 | async-start | bytes 262144 | tf_op jit(solution)/shard_map/all_to_all | solution.py:39
  70.4 0.7 constant_dynamic-update-slice_fusion.2
  71.1 0.7 constant_dynamic-update-slice_fusion.1
  71.8 0.7 constant_dynamic-update-slice_fusion
  72.4 7.1 %all-to-all-done.2 = bf16[16,2,2048]{2,1,0:T(2,128)(2,1)S(1)} async-done(((bf16[16,2,2048]{2,1,0:T(2,128)(2,1)}), bf16[16,2,2048]{2,1,0:T(2,128)(2,1)S(1)}, u32[]{:S(2)}, u32[]{:S(2)}) %all-to-all-start.2) | async-done | bytes 131104 | tf_op jit(solution)/shard_map/all_to_all | solution.py:39
  80.4 3.9 %fusion.2 = f32[1024,512]{1,0:T(8,128)S(1)} fusion(f32[1024,128]{1,0:T(8,128)S(1)} %fusion.10, bf16[2048,1024]{1,0:T(8,128)(2,1)} %all-gather.2.cloned.1.call-done, bf16[1,1,128,2048]{3,2,1,0:T(8,128)(2,1)} %param.11, bf16[1,1,512,128]{3,2,1,0:T(8,128)(2,1)S(1)} %copy-done.2), kind=kOutput, calls=%fused_computation.7 | convolution fusion | flops 671350784 | bytes 7471104 | tf_op jit(solution)/shard_map/dot_general | solution.py:94
  84.4 3.4 %fusion = bf16[1,1,512,1024]{2,3,1,0:T(8,128)(2,1)} fusion(f32[1024,512]{1,0:T(8,128)S(1)} %fusion.2, bf16[768,1024]{1,0:T(8,128)(2,1)} %constant_dynamic-update-slice_fusion, bf16[1,1,512,768]{3,2,1,0:T(8,128)(2,1)S(1)} %copy-done), kind=kOutput, calls=%fused_computation.2 | convolution fusion | flops 806354944 | bytes 5505024 | tf_op jit(solution)/shard_map/dot_general | solution.py:75
  87.8 2.3 %copy.15 = bf16[1,1,512,1024]{3,2,1,0:T(8,128)(2,1)} copy(bf16[1,1,512,1024]{2,3,1,0:T(8,128)(2,1)} %fusion) | data formatting | bytes 2097152 | tf_op jit(solution)/shard_map/reshape | solution.py:95
  (41 shorter events, 3.2 us)
Async XLA Ops:
  6.5 77.8 %copy-start = (bf16[1,1,512,768]{3,2,1,0:T(8,128)(2,1)S(1)}, bf16[1,1,512,768]{3,2,1,0:T(8,128)(2,1)}, u32[]{:S(2)}) copy-start(bf16[1,1,512,768]{3,2,1,0:T(8,128)(2,1)} %param.9) | copy-start | bytes 2359300
  6.5 2.4 %copy-start.4 = (bf16[1,1,128,64]{2,3,1,0:T(8,128)(2,1)S(1)}, bf16[1,1,128,64]{2,3,1,0:T(8,128)(2,1)}, u32[]{:S(2)}) copy-start(bf16[1,1,128,64]{2,3,1,0:T(8,128)(2,1)} %param.12) | copy-start | bytes 49156
  6.5 73.9 %all-gather.2.cloned.1.call-start = ((), (), s32[]{:S(2)}) async-start(), calls=%async_computation.3 | async-start | bytes 4456448 | tf_op jit(solution)/shard_map/all_gather | solution.py:51
  10.1 12.4 %copy-start.5 = (s32[1,1,4,64]{3,2,1,0:T(4,128)S(1)}, s32[1,1,4,64]{3,2,1,0:T(4,128)}, u32[]{:S(2)}) copy-start(s32[1,1,4,64]{3,2,1,0:T(4,128)} %param.8) | copy-start | bytes 3076
  10.1 12.6 %copy-start.1 = (bf16[1,1,512,1024]{3,2,1,0:T(8,128)(2,1)S(1)}, bf16[1,1,512,1024]{3,2,1,0:T(8,128)(2,1)}, u32[]{:S(2)}) copy-start(bf16[1,1,512,1024]{3,2,1,0:T(8,128)(2,1)} %param.7) | copy-start | bytes 3145732
  11.5 22.7 %all-to-all-start = ((f32[16,1,4096]{2,1,0:T(1,128)}), f32[16,1,4096]{2,1,0:T(1,128)S(1)}, u32[]{:S(2)}, u32[]{:S(2)}) async-start(f32[16,1,4096]{2,1,0:T(1,128)} %reshape.71), calls=%async_computation | async-start | bytes 524288 | tf_op jit(solution)/shard_map/all_to_all | solution.py:27
  37.3 24.1 %all-to-all-start.1 = ((bf16[32,2,2048]{2,1,0:T(2,128)(2,1)}), bf16[32,2,2048]{2,1,0:T(2,128)(2,1)S(1)}, u32[]{:S(2)}, u32[]{:S(2)}) async-start(bf16[32,2,2048]{2,1,0:T(2,128)(2,1)} %reshape.73), calls=%async_computation.1 | async-start | bytes 524288 | tf_op jit(solution)/shard_map/all_to_all | solution.py:39
  46.6 14.2 %collective-permute-start = (bf16[64,1024]{1,0:T(8,128)(2,1)S(1)}, bf16[64,1024]{1,0:T(8,128)(2,1)S(1)}, u32[]{:S(2)}, u32[]{:S(2)}) collective-permute-start(bf16[64,1024]{1,0:T(8,128)(2,1)S(1)} %get-tuple-element.8), channel_id=1, source_target_pairs={{0,32},{32,64},{64,96},{96,128},{128,160},{160,192},{192,224},{224... | collective-permute-start | bytes 393224 | tf_op jit(solution)/shard_map/ppermute | solution.py:14
  48.7 21.7 %collective-permute-start.1 = (bf16[64,1024]{1,0:T(8,128)(2,1)S(1)}, bf16[64,1024]{1,0:T(8,128)(2,1)S(1)}, u32[]{:S(2)}, u32[]{:S(2)}) collective-permute-start(bf16[64,1024]{1,0:T(8,128)(2,1)S(1)} %get-tuple-element.7), channel_id=1, source_target_pairs={{32,0},{64,32},{96,64},{128,96},{160,128},{192,160},{224,192},{256... | collective-permute-start | bytes 393224 | tf_op jit(solution)/shard_map/ppermute | solution.py:15
  51.0 20.1 %collective-permute-start.2 = (bf16[64,1024]{1,0:T(8,128)(2,1)S(1)}, bf16[64,1024]{1,0:T(8,128)(2,1)S(1)}, u32[]{:S(2)}, u32[]{:S(2)}) collective-permute-start(bf16[64,1024]{1,0:T(8,128)(2,1)S(1)} %get-tuple-element.6), channel_id=1, source_target_pairs={{0,1},{1,2},{2,3},{3,4},{4,5},{5,6},{6,7},{7,8},{8,9},{9,10},{10,1... | collective-permute-start | bytes 393224 | tf_op jit(solution)/shard_map/ppermute | solution.py:14
  54.1 7.8 %copy-start.3 = (bf16[1,64,2048]{2,1,0:T(8,128)(2,1)S(1)}, bf16[1,64,2048]{2,1,0:T(8,128)(2,1)}, u32[]{:S(2)}) copy-start(bf16[1,64,2048]{2,1,0:T(8,128)(2,1)} %param.13) | copy-start | bytes 786436
  54.1 17.7 %collective-permute-start.3 = (bf16[64,1024]{1,0:T(8,128)(2,1)S(1)}, bf16[64,1024]{1,0:T(8,128)(2,1)S(1)}, u32[]{:S(2)}, u32[]{:S(2)}) collective-permute-start(bf16[64,1024]{1,0:T(8,128)(2,1)S(1)} %get-tuple-element.5), channel_id=1, source_target_pairs={{1,0},{2,1},{3,2},{4,3},{5,4},{6,5},{7,6},{8,7},{9,8},{10,9},{11,1... | collective-permute-start | bytes 393224 | tf_op jit(solution)/shard_map/ppermute | solution.py:15
  63.2 17.2 %copy-start.2 = (bf16[1,1,512,128]{3,2,1,0:T(8,128)(2,1)S(1)}, bf16[1,1,512,128]{3,2,1,0:T(8,128)(2,1)}, u32[]{:S(2)}) copy-start(bf16[1,1,512,128]{3,2,1,0:T(8,128)(2,1)} %param.10) | copy-start | bytes 393220
  63.2 16.3 %all-to-all-start.2 = ((bf16[16,2,2048]{2,1,0:T(2,128)(2,1)}), bf16[16,2,2048]{2,1,0:T(2,128)(2,1)S(1)}, u32[]{:S(2)}, u32[]{:S(2)}) async-start(bf16[16,2,2048]{2,1,0:T(2,128)(2,1)} %reshape.75), calls=%async_computation.2 | async-start | bytes 262144 | tf_op jit(solution)/shard_map/all_to_all | solution.py:39
Sparse Core Ops, SparseCore 0:
  9.5 51.0 all-gather.1
where the time goes:
time: 97.4 us; the launch traced here: 96.9 us
  starting transfers between devices  40.5 us (42%)
  waiting for transfers between devices  17.4 us (18%)
  between operations  13.6 us (14%)
  local copies, waits for them, and re-layouts  12.7 us (13%)
  matrix products  11.4 us (12%)
  other arithmetic  1.35 us (1%)
    all_to_all x2, starting transfers between devices, sent_to_all(): lax.all_to_all(jnp.broadcast_to(shard[None], (devices, *shard.shape)), ax...  16.4 us
    all_to_all x1, starting transfers between devices, summed_on_arrival(): lax.all_to_all(blocks, axis, split_axis=0, concat_axis=0, tiled=True)  11 us
    all_to_all x1, waiting for transfers between devices, summed_on_arrival(): lax.all_to_all(blocks, axis, split_axis=0, concat_axis=0, tiled=True)  10.2 us
    ppermute x2, starting transfers between devices, extended(): after = lax.ppermute(leading, axis, down)  7.9 us
    all_to_all x2, waiting for transfers between devices, sent_to_all(): lax.all_to_all(jnp.broadcast_to(shard[None], (devices, *shard.shape)), ax...  7.12 us
    unnamed x22, local copies, waits for them, and re-layouts  6.95 us
    ppermute x2, starting transfers between devices, extended(): before = lax.ppermute(last, axis, up)  5.17 us
    dot_general x1, matrix products, per_device(): total = local + jnp.dot(basis, weights, preferred_element_type=jnp.float32)  3.89 us
  transfers between devices with their start and end apart: 8, of which 2 were waited for; matrix products, arithmetic and copies ran while one was open for 14% of the time, Pallas kernels for 0%

commit v1 on v0

v1 whole, which is shorter than its diff:
```python
import functools

import jax
import jax.numpy as jnp
from jax import lax
from jax.experimental import pallas as pl
from jax.experimental.pallas import tpu as pltpu
from jax.sharding import PartitionSpec as P

F32 = jnp.float32
BF16 = jnp.bfloat16
MESH = pl.DeviceIdType.MESH
NH = 2


def contract_rows(a, b):
    return lax.dot_general(a, b, (((0,), (0,)), ((), ())), preferred_element_type=F32)


def kernel(
    n_sub, n_region,
    res_hbm, rows_hbm, inv_hbm, basis_hbm, reg_hbm, map_hbm, root_hbm, out_hbm,
    res, rows, inv, basis, reginv, rmap, rootinv,
    xbuf, lent, margins, rs_send, rs_recv, gath, sols, regional, local, out,
    in_sem, out_sem, ring_send, ring_recv, share_send, share_recv,
    lent_send, lent_recv, rs_ss, rs_rs, pl_ss, pl_rs, so_ss, so_rs,
):
    s = lax.axis_index("sub")
    g = lax.axis_index("region")
    n_z = n_sub // 2
    z, c = s // 2, s % 2
    sib = s + 1 - 2 * c
    n_cols = res.shape[1]
    kc = basis.shape[1]
    wide = n_cols // NH

    loads = [
        pltpu.make_async_copy(a, b, in_sem.at[i])
        for i, (a, b) in enumerate(
            (
                (basis_hbm, basis), (res_hbm, res), (map_hbm, rmap), (rows_hbm, rows),
                (inv_hbm, inv), (root_hbm, rootinv), (reg_hbm, reginv),
            )
        )
    ]
    for load in loads:
        load.start()

    barrier = pltpu.get_barrier_semaphore()

    @pl.loop(1, n_sub)
    def _(k):
        pl.semaphore_signal(barrier, inc=1, device_id=(lax.rem(s + k, n_sub), g), device_id_type=MESH)

    @pl.loop(1, n_region)
    def _(k):
        pl.semaphore_signal(barrier, inc=1, device_id=(s, lax.rem(g + k, n_region)), device_id_type=MESH)

    core_rows = pl.ds(pl.multiple_of(c * kc, kc), kc)
    loads[0].wait()
    loads[1].wait()
    x = contract_rows(basis[...], res[...]).astype(BF16)
    xbuf[z, core_rows, :] = x

    loads[2].wait()
    proj = contract_rows(rmap[...], x)
    half = proj.shape[0] // 2
    low = lax.broadcasted_iota(jnp.int32, (half, 128), 1) < 64
    for zz in range(n_z):
        top = proj[:half, zz * 128:(zz + 1) * 128]
        bot = proj[half:, zz * 128:(zz + 1) * 128]
        rs_send[2 * zz] = jnp.where(low, top, pltpu.roll(bot, 64, 1))
        rs_send[2 * zz + 1] = jnp.where(low, pltpu.roll(top, 64, 1), bot)

    pl.semaphore_wait(barrier, n_sub - 1 + n_region - 1)

    def rs_copy(k):
        to = lax.rem(s + k, n_sub)
        return pltpu.make_async_remote_copy(
            rs_send.at[to], rs_recv.at[k - 1], rs_ss, rs_rs, device_id=(to, g), device_id_type=MESH
        )

    @pl.loop(1, n_sub)
    def _(k):
        rs_copy(k).start()

    def block(zz, h):
        return xbuf.at[zz, core_rows, pl.ds(h * wide, wide)]

    def ring(way, t, h):
        to = lax.rem(z + (1 if way == 0 else n_z - 1), n_z)
        zz = lax.rem(z + (n_z - t if way == 0 else t), n_z)
        ref = block(zz, h)
        return pltpu.make_async_remote_copy(
            ref, ref, ring_send.at[way, t, h], ring_recv.at[way, t, h],
            device_id=(2 * to + c, g), device_id_type=MESH,
        )

    def ring_arrived(way, t, h):
        zz = lax.rem(z + (n_z - t - 1 if way == 0 else t + 1), n_z)
        ref = block(zz, h)
        pltpu.make_async_copy(ref, ref, ring_recv.at[way, t, h]).wait()

    def share(d, h):
        ref = block(lax.rem(z + d, n_z), h)
        return pltpu.make_async_remote_copy(
            ref, ref, share_send.at[d, h], share_recv.at[d, h],
            device_id=(sib, g), device_id_type=MESH,
        )

    def shared_arrived(d, h):
        zz = lax.rem(z + d, n_z)
        ref = xbuf.at[zz, pl.ds(pl.multiple_of((1 - c) * kc, kc), kc), pl.ds(h * wide, wide)]
        pltpu.make_async_copy(ref, ref, share_recv.at[d, h]).wait()

    last = n_z // 2 - 1

    def goes(way, t, h):
        return t < last or (t == last and (h < NH // 2) == (way == 0))

    for h in range(NH):
        for way in range(2):
            ring(way, 0, h).start()
    for h in range(NH):
        share(0, h).start()

    loads[3].wait()
    owned = res.shape[0]
    margin = rows.shape[1]

    def lent_copy(j):
        to = ((s - 1, g), (s + 1, g), (s, g - 1), (s, g + 1))[j]
        place = (1, 0, 3, 2)[j]
        return pltpu.make_async_remote_copy(
            lent.at[pl.ds(j * margin, margin)], margins.at[pl.ds(place * margin, margin)],
            lent_send.at[j], lent_recv.at[place], device_id=to, device_id_type=MESH,
        )

    has = (s > 0, s < n_sub - 1, g > 0, g < n_region - 1)
    for j in range(4):
        row_id = lax.broadcasted_iota(jnp.int32, (owned, margin), 0)
        pick = jnp.where(row_id == rows[pl.ds(j, 1), :], 1.0, 0.0).astype(BF16)
        lent[pl.ds(j * margin, margin), :] = contract_rows(pick, res[...]).astype(BF16)

        @pl.when(has[j])
        def _():
            lent_copy(j).start()

        @pl.when(jnp.logical_not(has[j]))
        def _():
            margins[pl.ds(j * margin, margin), :] = jnp.zeros((margin, n_cols), BF16)

    pltpu.make_async_copy(rs_recv, rs_recv, rs_rs).wait()
    total = rs_send[s] + rs_recv[0]
    for k in range(1, n_sub - 1):
        total += rs_recv[k]
    gath[g] = total.astype(BF16)

    def plane_copy(k):
        to = lax.rem(g + k, n_region)
        return pltpu.make_async_remote_copy(
            gath.at[g], gath.at[g], pl_ss, pl_rs, device_id=(s, to), device_id_type=MESH
        )

    @pl.loop(1, n_region)
    def _(k):
        plane_copy(k).start()

    def step(t):
        for h in range(NH):
            for way in range(2):
                if goes(way, t, h):
                    ring_arrived(way, t, h)
                    if t < last and goes(way, t + 1, h):
                        ring(way, t + 1, h).start()
                    share(n_z - t - 1 if way == 0 else t + 1, h).start()

    def regional_block(d, first=False):
        zz = lax.rem(z + d, n_z)
        for h in range(NH):
            shared_arrived(d, h)
        part = jnp.dot(
            reginv[:, pl.ds(pl.multiple_of(zz * 2 * kc, 2 * kc), 2 * kc)], xbuf[zz],
            preferred_element_type=F32,
        )
        regional[...] = part if first else regional[...] + part

    step(0)
    loads[4].wait()
    local[...] = jnp.dot(inv[:, :owned], res[...], preferred_element_type=F32)
    loads[6].wait()
    regional_block(0, True)
    step(1)
    regional_block(1)
    regional_block(n_z - 1)

    loads[5].wait()
    others = gath.at[pl.ds(0, n_region - 1)]
    pltpu.make_async_copy(others, others, pl_rs).wait()
    packed = gath[...]
    lowb = lax.broadcasted_iota(jnp.int32, packed.shape, 2) < 64
    zero = jnp.zeros_like(packed)
    both = jnp.concatenate([jnp.where(lowb, packed, zero), jnp.where(lowb, zero, packed)], axis=1)
    sol = jnp.dot(rootinv[...], both.reshape(2 * half * n_region, 128), preferred_element_type=F32)
    sol = sol + pltpu.roll(sol, 64, 1)
    sols[s] = jnp.where(low, sol[:half], sol[half:]).astype(BF16)

    def sol_copy(k):
        to = lax.rem(s + k, n_sub)
        return pltpu.make_async_remote_copy(
            sols.at[s], sols.at[s], so_ss, so_rs, device_id=(to, g), device_id_type=MESH
        )

    @pl.loop(1, n_sub)
    def _(k):
        sol_copy(k).start()

    step(2)

    for j in range(4):
        @pl.when(has[j])
        def _():
            ref = margins.at[pl.ds(j * margin, margin)]
            pltpu.make_async_copy(ref, ref, lent_recv.at[j]).wait()

    local[...] += jnp.dot(inv[:, owned:], margins[...], preferred_element_type=F32)
    for d in (2, n_z - 2, 3, n_z - 3):
        regional_block(d)

    others_sol = sols.at[pl.ds(0, n_sub - 1)]
    pltpu.make_async_copy(others_sol, others_sol, so_rs).wait()
    for zz in range(n_z):
        p0 = sols[2 * zz].astype(F32)
        p1 = sols[2 * zz + 1].astype(F32)
        top = jnp.where(low, p0, pltpu.roll(p1, 64, 1))
        bot = jnp.where(low, pltpu.roll(p0, 64, 1), p1)
        rsol = jnp.concatenate([top, bot], axis=0).astype(BF16)
        cols = slice(zz * 128, (zz + 1) * 128)
        regional[:, cols] += jnp.dot(rmap[...], rsol, preferred_element_type=F32)

    step(3)
    regional_block(n_z // 2)

    n_out = 4
    stores = []
    for n in range(n_out):
        width = n_cols // n_out
        cols = slice(n * width, (n + 1) * width)
        w = regional[:, cols].astype(BF16)
        out[:, cols] = (
            local[:, cols] + jnp.dot(basis[...], w, preferred_element_type=F32)
        ).astype(BF16)
        store = pltpu.make_async_copy(
            out.at[:, pl.ds(n * width, width)], out_hbm.at[:, pl.ds(n * width, width)], out_sem.at[n]
        )
        store.start()
        stores.append(store)

    for h in range(NH):
        for way in range(2):
            for t in range(last + 1):
                if goes(way, t, h):
                    ring(way, t, h).wait_send()
        for d in range(n_z):
            share(d, h).wait_send()
    for j in range(4):
        @pl.when(has[j])
        def _():
            lent_copy(j).wait_send()
    pltpu.make_async_copy(rs_recv, rs_recv, rs_ss).wait()
    pltpu.make_async_copy(others, others, pl_ss).wait()
    pltpu.make_async_copy(others_sol, others_sol, so_ss).wait()
    for store in stores:
        store.wait()


def per_device(n_sub, n_region, residual, send_rows, local_inverse, coarse_basis, regional_inverse, root_map, root_inverse):
    args = (
        residual[0, 0], send_rows[0, 0], local_inverse[0, 0], coarse_basis[0, 0],
        regional_inverse[0, 0], root_map[0, 0], root_inverse[0],
    )
    res, rows, inv, basis, reginv, rmap, rootinv = args
    owned, cols = res.shape
    kc, kr = rmap.shape
    margin = rows.shape[1]
    n_z = n_sub // 2
    dma = pltpu.SemaphoreType.DMA
    flops = 2 * cols * (owned * inv.shape[1] + kc * reginv.shape[1] + 2 * kc * owned + 4 * kr * kc + 4 * margin * owned)
    out = pl.pallas_call(
        functools.partial(kernel, n_sub, n_region),
        out_shape=jax.ShapeDtypeStruct((owned, cols), BF16),
        in_specs=[pl.BlockSpec(memory_space=pl.ANY)] * 7,
        out_specs=pl.BlockSpec(memory_space=pl.ANY),
        scratch_shapes=[pltpu.VMEM(a.shape, a.dtype) for a in args]
        + [
            pltpu.VMEM((n_z, 2 * kc, cols), BF16),
            pltpu.VMEM((4 * margin, cols), BF16),
            pltpu.VMEM((4 * margin, cols), BF16),
            pltpu.VMEM((n_sub, kr // 2, 128), F32),
            pltpu.VMEM((n_sub - 1, kr // 2, 128), F32),
            pltpu.VMEM((n_region, kr // 2, 128), BF16),
            pltpu.VMEM((n_sub, kr // 2, 128), BF16),
            pltpu.VMEM((kc, cols), F32),
            pltpu.VMEM((owned, cols), F32),
            pltpu.VMEM((owned, cols), BF16),
            dma((7,)), dma((4,)),
            dma((2, n_z // 2, NH)), dma((2, n_z // 2, NH)),
            dma((n_z, NH)), dma((n_z, NH)),
            dma((4,)), dma((4,)),
            dma, dma, dma, dma, dma, dma,
        ],
        compiler_params=pltpu.CompilerParams(
            collective_id=0, has_side_effects=True, vmem_limit_bytes=48 * 1024 * 1024
        ),
        cost_estimate=pl.CostEstimate(flops=flops, bytes_accessed=4 << 20, transcendentals=0),
    )(*args)
    return out.reshape(1, 1, owned, cols)


def solution(mesh):
    here = P("sub", "region", None, None)
    return jax.shard_map(
        functools.partial(per_device, mesh.shape["sub"], mesh.shape["region"]),
        mesh=mesh,
        in_specs=(here,) * 6 + (P("region", None, None),),
        out_specs=here,
        check_vma=False,
    )
```

time: 97.4 us -> 59.1 us (0.61)
  the two profiles are of different devices: /device:TPU:33 before, /device:TPU:1 now
where the time goes in v1:
time: 59.1 us; the launch traced here: 58.8 us
  Pallas kernels  51.7 us (87%)
  local copies, waits for them, and re-layouts  7.06 us (12%)
    pallas_call x1, Pallas kernels, per_device(): pl.pallas_call(functools.partial(kernel, n_sub, n_region), out_shape=jax....  51.7 us
    unnamed x14, local copies, waits for them, and re-layouts  7.06 us

profile of v1, /device:TPU:1, one launch (start us, length us, event | category | flops | bytes accessed | tf_op | source)
XLA Modules:
  0.0 58.8 jit_solution(10318748663546021326)
XLA Ops:
  0.0 0.0 copy-start.5
  0.0 0.8 %copy.8 = bf16[1,1,128,64]{3,2,1,0:T(8,128)(2,1)S(1)} copy(bf16[1,1,128,64]{2,3,1,0:T(8,128)(2,1)} %param.12) | data formatting | bytes 32768 | tf_op args[5]
  0.8 0.0 copy-done.5
  0.9 0.0 copy-start
  0.9 1.2 %copy-done = bf16[1,1,512,1024]{3,2,1,0:T(8,128)(2,1)S(1)} copy-done((bf16[1,1,512,1024]{3,2,1,0:T(8,128)(2,1)S(1)}, bf16[1,1,512,1024]{3,2,1,0:T(8,128)(2,1)}, u32[]{:S(2)}) %copy-start) | copy-done | bytes 1048600
  2.1 0.0 copy-start.1
  2.1 1.1 %copy-done.1 = bf16[1,1,512,768]{3,2,1,0:T(8,128)(2,1)S(1)} copy-done((bf16[1,1,512,768]{3,2,1,0:T(8,128)(2,1)S(1)}, bf16[1,1,512,768]{3,2,1,0:T(8,128)(2,1)}, u32[]{:S(2)}) %copy-start.1) | copy-done | bytes 786456
  3.2 0.0 copy-start.2
  3.2 1.0 %copy-done.2 = bf16[1,1,128,2048]{3,2,1,0:T(8,128)(2,1)S(1)} copy-done((bf16[1,1,128,2048]{3,2,1,0:T(8,128)(2,1)S(1)}, bf16[1,1,128,2048]{3,2,1,0:T(8,128)(2,1)}, u32[]{:S(2)}) %copy-start.2) | copy-done | bytes 524312
  4.3 0.0 copy-start.3
  4.3 0.9 %copy-done.3 = bf16[1,64,2048]{2,1,0:T(8,128)(2,1)S(1)} copy-done((bf16[1,64,2048]{2,1,0:T(8,128)(2,1)S(1)}, bf16[1,64,2048]{2,1,0:T(8,128)(2,1)}, u32[]{:S(2)}) %copy-start.3) | copy-done | bytes 262168
  5.2 0.0 copy-start.4
  5.2 0.9 %copy-done.4 = bf16[1,1,512,128]{3,2,1,0:T(8,128)(2,1)S(1)} copy-done((bf16[1,1,512,128]{3,2,1,0:T(8,128)(2,1)S(1)}, bf16[1,1,512,128]{3,2,1,0:T(8,128)(2,1)}, u32[]{:S(2)}) %copy-start.4) | copy-done | bytes 131096
  6.1 51.7 %shard_map.73 = bf16[512,1024]{1,0:T(8,128)(2,1)S(1)} custom-call(bf16[512,1024]{1,0:T(8,128)(2,1)S(1)} %bitcast.10, s32[4,64]{1,0:T(4,128)S(1)} %bitcast.15, bf16[512,768]{1,0:T(8,128)(2,1)S(1)} %bitcast.11, bf16[512,128]{1,0:T(8,128)(2,1)S(1)} %bitcast.14, bf16[128,2048]{1,0:T(8,128)(2,1)S(1)} %bitcast.12, bf16[128,64]{1,0:T(8,128)(2,1)S(1)} %bitcast.9, ...), custom_call_target="tpu_custom_call" | custom-call | flops 1946157056 | bytes 4194304 | tf_op jit(solution)/shard_map/pallas_call | solution.py:289
  57.8 1.0 %copy.10 = bf16[1,1,512,1024]{3,2,1,0:T(8,128)(2,1)} copy(bf16[1,1,512,1024]{3,2,1,0:T(8,128)(2,1)S(1)} %bitcast.8) | data formatting | bytes 2097152
Async XLA Ops:
  0.0 0.8 %copy-start.5 = (s32[1,1,4,64]{3,2,1,0:T(4,128)S(1)}, s32[1,1,4,64]{3,2,1,0:T(4,128)}, u32[]{:S(2)}) copy-start(s32[1,1,4,64]{3,2,1,0:T(4,128)} %param.8) | copy-start | bytes 3076
  0.9 1.2 %copy-start = (bf16[1,1,512,1024]{3,2,1,0:T(8,128)(2,1)S(1)}, bf16[1,1,512,1024]{3,2,1,0:T(8,128)(2,1)}, u32[]{:S(2)}) copy-start(bf16[1,1,512,1024]{3,2,1,0:T(8,128)(2,1)} %param.7) | copy-start | bytes 3145732
  2.1 1.1 %copy-start.1 = (bf16[1,1,512,768]{3,2,1,0:T(8,128)(2,1)S(1)}, bf16[1,1,512,768]{3,2,1,0:T(8,128)(2,1)}, u32[]{:S(2)}) copy-start(bf16[1,1,512,768]{3,2,1,0:T(8,128)(2,1)} %param.9) | copy-start | bytes 2359300
  3.2 1.0 %copy-start.2 = (bf16[1,1,128,2048]{3,2,1,0:T(8,128)(2,1)S(1)}, bf16[1,1,128,2048]{3,2,1,0:T(8,128)(2,1)}, u32[]{:S(2)}) copy-start(bf16[1,1,128,2048]{3,2,1,0:T(8,128)(2,1)} %param.11) | copy-start | bytes 1572868
  4.3 0.9 %copy-start.3 = (bf16[1,64,2048]{2,1,0:T(8,128)(2,1)S(1)}, bf16[1,64,2048]{2,1,0:T(8,128)(2,1)}, u32[]{:S(2)}) copy-start(bf16[1,64,2048]{2,1,0:T(8,128)(2,1)} %param.13) | copy-start | bytes 786436
  5.2 0.9 %copy-start.4 = (bf16[1,1,512,128]{3,2,1,0:T(8,128)(2,1)S(1)}, bf16[1,1,512,128]{3,2,1,0:T(8,128)(2,1)}, u32[]{:S(2)}) copy-start(bf16[1,1,512,128]{3,2,1,0:T(8,128)(2,1)} %param.10) | copy-start | bytes 393220

commit v2 on v1

v2 whole, which is shorter than its diff:
```python
import functools

import jax
import jax.numpy as jnp
from jax import lax
from jax.experimental import pallas as pl
from jax.experimental.pallas import tpu as pltpu
from jax.sharding import PartitionSpec as P

F32 = jnp.float32
BF16 = jnp.bfloat16
MESH = pl.DeviceIdType.MESH
NH = 2
NX = 4


def contract_rows(a, b):
    return lax.dot_general(a, b, (((0,), (0,)), ((), ())), preferred_element_type=F32)


def kernel(
    n_sub, n_region,
    res_hbm, rows_hbm, inv_hbm, basis_hbm, reg_hbm, map_hbm, root_hbm, out_hbm,
    res, rows, inv, basis, reginv, rmap, rootinv,
    xbuf, lent, margins, rs_part, rs_pair, rs_chip, rs_send, rs_recv, gath, sols, regional, local, out,
    in_sem, out_sem, ring_send, ring_recv, share_send, share_recv,
    lent_send, lent_recv, rs_ss, rs_rs, py_ss, py_rs, px_ss, px_rs, so_ss, so_rs,
    pair_sem, ready_near, ready_col, ready_plane,
):
    s = lax.axis_index("sub")
    g = lax.axis_index("region")
    n_z = n_sub // 2
    n_y = n_region // NX
    z, c = s // 2, s % 2
    y, xx = g // NX, g % NX
    sib = s + 1 - 2 * c
    n_cols = res.shape[1]
    kc = basis.shape[1]
    wide = n_cols // NH
    margin = rows.shape[1]
    owned = res.shape[0]

    def piece(ref, h):
        return ref.at[:, pl.ds(h * wide, wide)]

    basis_load = pltpu.make_async_copy(basis_hbm, basis, in_sem.at[0])
    res_loads = [pltpu.make_async_copy(piece(res_hbm, h), piece(res, h), in_sem.at[1 + h]) for h in range(NH)]
    map_load, rows_load, inv_load, reg_load, root_load = [
        pltpu.make_async_copy(a, b, in_sem.at[1 + NH + i])
        for i, (a, b) in enumerate(
            ((map_hbm, rmap), (rows_hbm, rows), (inv_hbm, inv), (reg_hbm, reginv), (root_hbm, rootinv))
        )
    ]
    for load in (basis_load, *res_loads, map_load, rows_load, inv_load, reg_load, root_load):
        load.start()

    barrier = pltpu.get_barrier_semaphore()

    def signal(sem, to):
        pl.semaphore_signal(sem, inc=1, device_id=to, device_id_type=MESH)

    def wait_for(sem, n):
        pl.when(n > 0)(lambda: pl.semaphore_wait(sem, n))

    def y_rank(v):
        far = jnp.minimum(v, n_y - v)
        return jnp.where(v == 0, 0, 2 * far - 1 + jnp.where(v > n_y // 2, 1, 0))

    my_rank = y_rank(y)
    before_far = jnp.logical_and(xx == 0, y > 0)
    after_far = jnp.logical_and(xx == NX - 1, y < n_y - 1)
    plane = [((s, v * NX + xx), y != v, y_rank(v) > my_rank) for v in range(n_y)]
    plane += [((s, y * NX + v), xx != v, xx < v) for v in range(NX)]
    plane += [
        ((s, g - 1), before_far, y_rank(y - 1) > my_rank),
        ((s, g + 1), after_far, y_rank(y + 1) > my_rank),
    ]
    higher = [jnp.logical_and(there, up) for _, there, up in plane]
    lower = [jnp.logical_and(there, jnp.logical_not(up)) for _, there, up in plane]

    def count(flags):
        return sum(jnp.where(f, 1, 0) for f in flags)

    @pl.loop(z + 1, n_z)
    def _(to):
        signal(barrier, (2 * to + c, g))

    pl.when(c == 0)(lambda: signal(barrier, (sib, g)))
    across_down = jnp.logical_and(c == 0, z > 0)
    across_up = jnp.logical_and(c == 1, z < n_z - 1)
    pl.when(across_up)(lambda: signal(barrier, (s + 1, g)))

    for (to, _, _), up in zip(plane, higher):
        @pl.when(up)
        def _():
            signal(barrier, to)

    wait_for(barrier, z + c + count([across_down, *lower]))

    pl.when(z > 0)(lambda: signal(ready_near, (s - 2, g)))
    pl.when(c == 1)(lambda: signal(ready_near, (sib, g)))

    @pl.loop(0, z - 1)
    def _(to):
        signal(ready_col, (2 * to + c, g))

    pl.when(across_down)(lambda: signal(ready_col, (s - 1, g)))

    for (to, _, _), low_one in zip(plane, lower):
        @pl.when(low_one)
        def _():
            signal(ready_plane, to)

    n_near = count([z < n_z - 1, c == 0])
    n_far = jnp.maximum(n_z - 2 - z, 0) + count([across_up])

    core_rows = pl.ds(pl.multiple_of(c * kc, kc), kc)

    def block(zz, h):
        return xbuf.at[zz, core_rows, pl.ds(h * wide, wide)]

    def ring(way, t, h):
        to = lax.rem(z + (1 if way == 0 else n_z - 1), n_z)
        zz = lax.rem(z + (n_z - t if way == 0 else t), n_z)
        ref = block(zz, h)
        return pltpu.make_async_remote_copy(
            ref, ref, ring_send.at[way, t, h], ring_recv.at[way, t, h],
            device_id=(2 * to + c, g), device_id_type=MESH,
        )

    def ring_arrived(way, t, h):
        zz = lax.rem(z + (n_z - t - 1 if way == 0 else t + 1), n_z)
        ref = block(zz, h)
        pltpu.make_async_copy(ref, ref, ring_recv.at[way, t, h]).wait()

    def share(d, h):
        ref = block(lax.rem(z + d, n_z), h)
        return pltpu.make_async_remote_copy(
            ref, ref, share_send.at[d, h], share_recv.at[d, h],
            device_id=(sib, g), device_id_type=MESH,
        )

    def shared_arrived(d, h):
        zz = lax.rem(z + d, n_z)
        ref = xbuf.at[zz, pl.ds(pl.multiple_of((1 - c) * kc, kc), kc), pl.ds(h * wide, wide)]
        pltpu.make_async_copy(ref, ref, share_recv.at[d, h]).wait()

    last = n_z // 2 - 1

    def takes(way, t, h, to):
        if t < last:
            return None
        if (h < NH // 2) == (way == 0):
            return None if way == 1 else to != 0
        return to == 0 if way == 1 else False

    def when(cond, then):
        if cond is None:
            then()
        elif cond is not False:
            pl.when(cond)(then)

    chip_to = (lax.rem(z + 1, n_z), lax.rem(z + n_z - 1, n_z))

    basis_load.wait()
    for h in range(NH):
        res_loads[h].wait()
        cols = slice(h * wide, (h + 1) * wide)
        xbuf[z, core_rows, cols] = contract_rows(basis[...], res[:, cols]).astype(BF16)
        if h == 0:
            wait_for(ready_near, n_near)
            ring(0, 0, 0).start()
            pl.when(z > 0)(lambda: ring(1, 0, 0).start())
        share(0, h).start()

    map_load.wait()
    proj = jnp.dot(rmap[...], xbuf[z, core_rows, :], preferred_element_type=F32)
    half = proj.shape[0] // 2
    low = lax.broadcasted_iota(jnp.int32, (half, 128), 1) < 64
    for zz in range(n_z):
        top = proj[:half, zz * 128:(zz + 1) * 128]
        bot = proj[half:, zz * 128:(zz + 1) * 128]
        rs_part[0, zz] = jnp.where(low, top, pltpu.roll(bot, 64, 1))
        rs_part[1, zz] = jnp.where(low, pltpu.roll(top, 64, 1), bot)

    pair = pltpu.make_async_remote_copy(
        rs_part.at[1 - c], rs_pair, pair_sem.at[0], pair_sem.at[1], device_id=(sib, g), device_id_type=MESH
    )
    pair.start()
    pair.wait_recv()
    rs_chip[...] = rs_part[c] + rs_pair[...]
    rs_send[...] = rs_chip[...].astype(BF16)

    def rs_copy(to):
        return pltpu.make_async_remote_copy(
            rs_send.at[to], rs_recv.at[lax.rem(to - z + n_z, n_z) - 1], rs_ss, rs_rs,
            device_id=(2 * to + c, g), device_id_type=MESH,
        )

    @pl.loop(0, z)
    def _(to):
        rs_copy(to).start()

    def follow(way):
        for h in range(1, NH):
            ring(way, 0, h - 1).wait_send()
            ring(way, 0, h).start()

    follow(0)
    pl.when(z > 0)(lambda: follow(1))
    wait_for(ready_col, n_far)

    @pl.when(z == 0)
    def _():
        ring(1, 0, 0).start()

    @pl.loop(z + 1, n_z)
    def _(to):
        rs_copy(to).start()

    rows_load.wait()

    def lent_copy(j):
        to = ((s - 1, g), (s + 1, g), (s, g - 1), (s, g + 1))[j]
        place = (1, 0, 3, 2)[j]
        return pltpu.make_async_remote_copy(
            lent.at[pl.ds(j * margin, margin)], margins.at[pl.ds(place * margin, margin)],
            lent_send.at[j], lent_recv.at[place], device_id=to, device_id_type=MESH,
        )

    has = (s > 0, s < n_sub - 1, g > 0, g < n_region - 1)
    for j in range(4):
        if j == 2:
            wait_for(ready_plane, count(higher))
        row_id = lax.broadcasted_iota(jnp.int32, (owned, margin), 0)
        pick = jnp.where(row_id == rows[pl.ds(j, 1), :], 1.0, 0.0).astype(BF16)
        lent[pl.ds(j * margin, margin), :] = contract_rows(pick, res[...]).astype(BF16)

        @pl.when(has[j])
        def _():
            lent_copy(j).start()

        @pl.when(jnp.logical_not(has[j]))
        def _():
            margins[pl.ds(j * margin, margin), :] = jnp.zeros((margin, n_cols), BF16)

    pl.when(z == 0)(lambda: follow(1))

    inv_load.wait()
    local[...] = jnp.dot(inv[:, :owned], res[...], preferred_element_type=F32)

    def step(t, pieces=range(NH)):
        for h in pieces:
            for way in range(2):
                def arrived():
                    ring_arrived(way, t, h)
                    if t < last:
                        when(takes(way, t + 1, h, chip_to[way]), lambda: ring(way, t + 1, h).start())
                    share(n_z - t - 1 if way == 0 else t + 1, h).start()

                when(takes(way, t, h, z), arrived)

    def regional_block(d, first=False):
        zz = lax.rem(z + d, n_z)
        for h in range(NH):
            shared_arrived(d, h)
        part = jnp.dot(
            reginv[:, pl.ds(pl.multiple_of(zz * 2 * kc, 2 * kc), 2 * kc)], xbuf[zz],
            preferred_element_type=F32,
        )
        regional[...] = part if first else regional[...] + part

    reg_load.wait()
    regional_block(0, True)
    step(0)

    pltpu.make_async_copy(rs_recv, rs_recv, rs_rs).wait()
    total = rs_chip[z]
    for k in range(n_z - 1):
        total += rs_recv[k].astype(F32)
    gath[xx, y] = total.astype(BF16)

    def y_copy(k):
        to = lax.rem(y + k, n_y)
        return pltpu.make_async_remote_copy(
            gath.at[xx, y], gath.at[xx, y], py_ss, py_rs, device_id=(s, to * NX + xx), device_id_type=MESH
        )

    def x_copy(k):
        to = lax.rem(xx + k, NX)
        return pltpu.make_async_remote_copy(
            gath.at[xx], gath.at[xx], px_ss, px_rs, device_id=(s, y * NX + to), device_id_type=MESH
        )

    for k in range(1, n_y):
        y_copy(k).start()

    regional_block(1)
    regional_block(n_z - 1)
    step(1, range(NH // 2))

    others_y = gath.at[0, pl.ds(0, n_y - 1)]
    pltpu.make_async_copy(others_y, others_y, py_rs).wait()
    for k in range(1, NX):
        x_copy(k).start()

    step(1, range(NH // 2, NH))
    regional_block(2)
    regional_block(n_z - 2)

    root_load.wait()
    others_x = gath.at[pl.ds(0, NX - 1)]
    pltpu.make_async_copy(others_x, others_x, px_rs).wait()
    zero = jnp.zeros((half, 128), BF16)
    lowb = lax.broadcasted_iota(jnp.int32, (half, 128), 1) < 64
    both = []
    for v in range(n_y):
        for u in range(NX):
            packed = gath[u, v]
            both += [jnp.where(lowb, packed, zero), jnp.where(lowb, zero, packed)]
    sol = jnp.dot(rootinv[...], jnp.concatenate(both, axis=0), preferred_element_type=F32)
    sol = sol + pltpu.roll(sol, 64, 1)
    sols[c, z] = jnp.where(low, sol[:half], sol[half:]).astype(BF16)

    def sol_copy(k):
        to = lax.rem(z + k, n_z)
        return pltpu.make_async_remote_copy(
            sols.at[c, z], sols.at[c, z], so_ss, so_rs, device_id=(2 * to + c, g), device_id_type=MESH
        )

    @pl.loop(1, n_z)
    def _(k):
        sol_copy(k).start()

    step(2)

    for j in range(4):
        @pl.when(has[j])
        def _():
            ref = margins.at[pl.ds(j * margin, margin)]
            pltpu.make_async_copy(ref, ref, lent_recv.at[j]).wait()

    local[...] += jnp.dot(inv[:, owned:], margins[...], preferred_element_type=F32)
    for d in (3, n_z - 3):
        regional_block(d)

    others_sol = sols.at[0, pl.ds(0, n_z - 1)]
    pltpu.make_async_copy(others_sol, others_sol, so_rs).wait()
    sol_pair = pltpu.make_async_remote_copy(
        sols.at[c], sols.at[c], pair_sem.at[2], pair_sem.at[3], device_id=(sib, g), device_id_type=MESH
    )
    sol_pair.start()
    other_core = sols.at[1 - c]
    pltpu.make_async_copy(other_core, other_core, pair_sem.at[3]).wait()
    for zz in range(n_z):
        p0 = sols[0, zz].astype(F32)
        p1 = sols[1, zz].astype(F32)
        top = jnp.where(low, p0, pltpu.roll(p1, 64, 1))
        bot = jnp.where(low, pltpu.roll(p0, 64, 1), p1)
        rsol = jnp.concatenate([top, bot], axis=0).astype(BF16)
        cols = slice(zz * 128, (zz + 1) * 128)
        regional[:, cols] += contract_rows(rmap[...], rsol)

    step(3)
    regional_block(n_z // 2)

    n_out = 4
    stores = []
    for n in range(n_out):
        width = n_cols // n_out
        cols = slice(n * width, (n + 1) * width)
        w = regional[:, cols].astype(BF16)
        out[:, cols] = (
            local[:, cols] + jnp.dot(basis[...], w, preferred_element_type=F32)
        ).astype(BF16)
        store = pltpu.make_async_copy(
            out.at[:, pl.ds(n * width, width)], out_hbm.at[:, pl.ds(n * width, width)], out_sem.at[n]
        )
        store.start()
        stores.append(store)

    for h in range(NH):
        for way in range(2):
            for t in range(last + 1):
                if t > 0 or h == NH - 1:
                    when(takes(way, t, h, chip_to[way]), lambda: ring(way, t, h).wait_send())
        for d in range(n_z):
            share(d, h).wait_send()
    for j in range(4):
        @pl.when(has[j])
        def _():
            lent_copy(j).wait_send()
    pltpu.make_async_copy(rs_recv, rs_recv, rs_ss).wait()
    pair.wait_send()
    sol_pair.wait_send()
    pltpu.make_async_copy(others_y, others_y, py_ss).wait()
    pltpu.make_async_copy(others_x, others_x, px_ss).wait()
    pltpu.make_async_copy(others_sol, others_sol, so_ss).wait()
    for store in stores:
        store.wait()


def per_device(n_sub, n_region, residual, send_rows, local_inverse, coarse_basis, regional_inverse, root_map, root_inverse):
    args = (
        residual[0, 0], send_rows[0, 0], local_inverse[0, 0], coarse_basis[0, 0],
        regional_inverse[0, 0], root_map[0, 0].T, root_inverse[0],
    )
    res, rows, inv, basis, reginv, rmap, rootinv = args
    owned, cols = res.shape
    kr, kc = rmap.shape
    margin = rows.shape[1]
    n_z = n_sub // 2
    dma = pltpu.SemaphoreType.DMA
    flops = 2 * cols * (owned * inv.shape[1] + kc * reginv.shape[1] + 2 * kc * owned + 4 * kr * kc + 4 * margin * owned)
    out = pl.pallas_call(
        functools.partial(kernel, n_sub, n_region),
        out_shape=jax.ShapeDtypeStruct((owned, cols), BF16),
        in_specs=[pl.BlockSpec(memory_space=pl.ANY)] * 7,
        out_specs=pl.BlockSpec(memory_space=pl.ANY),
        scratch_shapes=[pltpu.VMEM(a.shape, a.dtype) for a in args]
        + [
            pltpu.VMEM((n_z, 2 * kc, cols), BF16),
            pltpu.VMEM((4 * margin, cols), BF16),
            pltpu.VMEM((4 * margin, cols), BF16),
            pltpu.VMEM((2, n_z, kr // 2, 128), F32),
            pltpu.VMEM((n_z, kr // 2, 128), F32),
            pltpu.VMEM((n_z, kr // 2, 128), F32),
            pltpu.VMEM((n_z, kr // 2, 128), BF16),
            pltpu.VMEM((n_z - 1, kr // 2, 128), BF16),
            pltpu.VMEM((NX, n_region // NX, kr // 2, 128), BF16),
            pltpu.VMEM((2, n_z, kr // 2, 128), BF16),
            pltpu.VMEM((kc, cols), F32),
            pltpu.VMEM((owned, cols), F32),
            pltpu.VMEM((owned, cols), BF16),
            dma((6 + NH,)), dma((4,)),
            dma((2, n_z // 2, NH)), dma((2, n_z // 2, NH)),
            dma((n_z, NH)), dma((n_z, NH)),
            dma((4,)), dma((4,)),
            *[dma] * 8,
            dma((4,)),
            *[pltpu.SemaphoreType.REGULAR] * 3,
        ],
        compiler_params=pltpu.CompilerParams(
            collective_id=0, has_side_effects=True, vmem_limit_bytes=60 * 1024 * 1024
        ),
        cost_estimate=pl.CostEstimate(flops=flops, bytes_accessed=4 << 20, transcendentals=0),
    )(*args)
    return out.reshape(1, 1, owned, cols)


def solution(mesh):
    here = P("sub", "region", None, None)
    return jax.shard_map(
        functools.partial(per_device, mesh.shape["sub"], mesh.shape["region"]),
        mesh=mesh,
        in_specs=(here,) * 6 + (P("region", None, None),),
        out_specs=here,
        check_vma=False,
    )
```

time: 59.1 us -> 46.4 us (0.79)
  Pallas kernels: 51.7 us -> 44 us
  local copies, waits for them, and re-layouts: 7.06 us -> 2.26 us
    pallas_call x1, Pallas kernels: 51.7 us -> 44 us  [per_device(): pl.pallas_call(functools.partial(kernel, n_sub, n_region), out_shape=jax....]
    unnamed x14 -> x1, local copies, waits for them, and re-layouts: 7.06 us -> 2.26 us
where the time goes in v2:
time: 46.4 us; the launch traced here: 46.3 us
  Pallas kernels  44 us (95%)
  local copies, waits for them, and re-layouts  2.26 us (5%)
    pallas_call x1, Pallas kernels, per_device(): pl.pallas_call(functools.partial(kernel, n_sub, n_region), out_shape=jax....  44 us
    unnamed x1, local copies, waits for them, and re-layouts  2.26 us

profile of v2, /device:TPU:1, one launch (start us, length us, event | category | flops | bytes accessed | tf_op | source)
XLA Modules:
  0.0 46.3 jit_solution(4717693392702495593)
XLA Ops:
  0.0 44.0 %shard_map.73 = bf16[512,1024]{1,0:T(8,128)(2,1)} custom-call(bf16[512,1024]{1,0:T(8,128)(2,1)} %bitcast.11, s32[4,64]{1,0:T(4,128)} %bitcast.17, bf16[512,768]{1,0:T(8,128)(2,1)} %bitcast.12, bf16[512,128]{1,0:T(8,128)(2,1)} %bitcast.15, bf16[128,2048]{1,0:T(8,128)(2,1)} %bitcast.13, bf16[64,128]{1,0:T(8,128)(2,1)} %bitcast.16, bf16[64,2048]{1,0:T(8,128)(2,1)} %bitcast.14), custom_call_target="tpu_custom_call" | custom-call | flops 1946157056 | bytes 4194304 | tf_op jit(solution)/shard_map/pallas_call | solution.py:415
  44.0 2.3 %copy.9 = bf16[1,1,512,1024]{3,2,1,0:T(8,128)(2,1)} copy(bf16[1,1,512,1024]{3,2,1,0:T(8,128)(2,1)} %bitcast.10) | data formatting | bytes 2097152

commit v3 on v2

--- a/solution.py
+++ b/solution.py
@@ -278,21 +278,32 @@
     total = rs_chip[z]
     for k in range(n_z - 1):
         total += rs_recv[k].astype(F32)
-    gath[xx, y] = total.astype(BF16)
+    gath[xx, 0] = total.astype(BF16)
+
+    by_distance = sorted(range(n_y), key=lambda d: (min(d, n_y - d), d))
+    place_of = {d: n for n, d in enumerate(by_distance)}
+    n_near_y = n_y // 2 + 1
+
+    def near(k):
+        return place_of[k] < n_near_y
 
     def y_copy(k):
         to = lax.rem(y + k, n_y)
         return pltpu.make_async_remote_copy(
-            gath.at[xx, y], gath.at[xx, y], py_ss, py_rs, device_id=(s, to * NX + xx), device_id_type=MESH
-        )
-
-    def x_copy(k):
+            gath.at[xx, 0], gath.at[xx, place_of[n_y - k]], py_ss, py_rs.at[0 if near(k) else 1],
+            device_id=(s, to * NX + xx), device_id_type=MESH,
+        )
+
+    groups = (pl.ds(0, n_near_y), pl.ds(n_near_y, n_y - n_near_y))
+
+    def x_copy(k, part):
         to = lax.rem(xx + k, NX)
-        return pltpu.make_async_remote_copy(
-            gath.at[xx], gath.at[xx], px_ss, px_rs, device_id=(s, y * NX + to), device_id_type=MESH
-        )
-
-    for k in range(1, n_y):
+        ref = gath.at[xx, groups[part]]
+        return pltpu.make_async_remote_copy(
+            ref, ref, px_ss, px_rs, device_id=(s, y * NX + to), device_id_type=MESH
+        )
+
+    for k in by_distance[1:]:
         y_copy(k).start()
 
     regional_block(1)
@@ -300,9 +311,11 @@
     step(1, range(NH // 2))
 
     others_y = gath.at[0, pl.ds(0, n_y - 1)]
-    pltpu.make_async_copy(others_y, others_y, py_rs).wait()
-    for k in range(1, NX):
-        x_copy(k).start()
+    for part, first in enumerate((1, n_near_y)):
+        arrived_y = gath.at[0, pl.ds(first, (n_near_y if part == 0 else n_y) - first)]
+        pltpu.make_async_copy(arrived_y, arrived_y, py_rs.at[part]).wait()
+        for k in range(1, NX):
+            x_copy(k, part).start()
 
     step(1, range(NH // 2, NH))
     regional_block(2)
@@ -316,7 +329,7 @@
     both = []
     for v in range(n_y):
         for u in range(NX):
-            packed = gath[u, v]
+            packed = gath[u, y_rank(lax.rem(v - y + n_y, n_y))]
             both += [jnp.where(lowb, packed, zero), jnp.where(lowb, zero, packed)]
     sol = jnp.dot(rootinv[...], jnp.concatenate(both, axis=0), preferred_element_type=F32)
     sol = sol + pltpu.roll(sol, 64, 1)
@@ -343,6 +356,8 @@
     local[...] += jnp.dot(inv[:, owned:], margins[...], preferred_element_type=F32)
     for d in (3, n_z - 3):
         regional_block(d)
+
+    step(3)
 
     others_sol = sols.at[0, pl.ds(0, n_z - 1)]
     pltpu.make_async_copy(others_sol, others_sol, so_rs).wait()
@@ -350,6 +365,7 @@
         sols.at[c], sols.at[c], pair_sem.at[2], pair_sem.at[3], device_id=(sib, g), device_id_type=MESH
     )
     sol_pair.start()
+    regional_block(n_z // 2)
     other_core = sols.at[1 - c]
     pltpu.make_async_copy(other_core, other_core, pair_sem.at[3]).wait()
     for zz in range(n_z):
@@ -360,9 +376,6 @@
         rsol = jnp.concatenate([top, bot], axis=0).astype(BF16)
         cols = slice(zz * 128, (zz + 1) * 128)
         regional[:, cols] += contract_rows(rmap[...], rsol)
-
-    step(3)
-    regional_block(n_z // 2)
 
     n_out = 4
     stores = []
@@ -436,7 +449,7 @@
             dma((2, n_z // 2, NH)), dma((2, n_z // 2, NH)),
             dma((n_z, NH)), dma((n_z, NH)),
             dma((4,)), dma((4,)),
-            *[dma] * 8,
+            *[dma] * 3, dma((2,)), *[dma] * 4,
             dma((4,)),
             *[pltpu.SemaphoreType.REGULAR] * 3,
         ],

time: 46.4 us -> 45 us (0.970)
  Pallas kernels: 44 us -> 42.6 us
    pallas_call x1, Pallas kernels: 44 us -> 42.6 us  [per_device(): pl.pallas_call(functools.partial(kernel, n_sub, n_region), out_shape=jax....]
where the time goes in v3:
time: 45 us; the launch traced here: 44.8 us
  Pallas kernels  42.6 us (95%)
  local copies, waits for them, and re-layouts  2.26 us (5%)
    pallas_call x1, Pallas kernels, per_device(): pl.pallas_call(functools.partial(kernel, n_sub, n_region), out_shape=jax....  42.6 us
    unnamed x1, local copies, waits for them, and re-layouts  2.26 us

profile of v3, /device:TPU:1, one launch (start us, length us, event | category | flops | bytes accessed | tf_op | source)
XLA Modules:
  0.0 44.8 jit_solution(1504784751729764072)
XLA Ops:
  0.0 42.6 %shard_map.73 = bf16[512,1024]{1,0:T(8,128)(2,1)} custom-call(bf16[512,1024]{1,0:T(8,128)(2,1)} %bitcast.11, s32[4,64]{1,0:T(4,128)} %bitcast.17, bf16[512,768]{1,0:T(8,128)(2,1)} %bitcast.12, bf16[512,128]{1,0:T(8,128)(2,1)} %bitcast.15, bf16[128,2048]{1,0:T(8,128)(2,1)} %bitcast.13, bf16[64,128]{1,0:T(8,128)(2,1)} %bitcast.16, bf16[64,2048]{1,0:T(8,128)(2,1)} %bitcast.14), custom_call_target="tpu_custom_call" | custom-call | flops 1946157056 | bytes 4194304 | tf_op jit(solution)/shard_map/pallas_call | solution.py:428
  42.6 2.3 %copy.9 = bf16[1,1,512,1024]{3,2,1,0:T(8,128)(2,1)} copy(bf16[1,1,512,1024]{3,2,1,0:T(8,128)(2,1)} %bitcast.10) | data formatting | bytes 2097152

commit v4 on v3

--- a/solution.py
+++ b/solution.py
@@ -251,7 +251,7 @@
 
     def step(t, pieces=range(NH)):
         for h in pieces:
-            for way in range(2):
+            for way in (1, 0):
                 def arrived():
                     ring_arrived(way, t, h)
                     if t < last:

time: 45 us -> 45 us (level)
  no operation moved by 1% of the time
where the time goes in v4:
time: 45 us; the launch traced here: 44.8 us
  Pallas kernels  42.6 us (95%)
  local copies, waits for them, and re-layouts  2.26 us (5%)
    pallas_call x1, Pallas kernels, per_device(): pl.pallas_call(functools.partial(kernel, n_sub, n_region), out_shape=jax....  42.6 us
    unnamed x1, local copies, waits for them, and re-layouts  2.26 us

profile of v4, /device:TPU:1, one launch (start us, length us, event | category | flops | bytes accessed | tf_op | source)
XLA Modules:
  0.0 44.8 jit_solution(18160611114836160593)
XLA Ops:
  0.0 42.6 %shard_map.73 = bf16[512,1024]{1,0:T(8,128)(2,1)} custom-call(bf16[512,1024]{1,0:T(8,128)(2,1)} %bitcast.11, s32[4,64]{1,0:T(4,128)} %bitcast.17, bf16[512,768]{1,0:T(8,128)(2,1)} %bitcast.12, bf16[512,128]{1,0:T(8,128)(2,1)} %bitcast.15, bf16[128,2048]{1,0:T(8,128)(2,1)} %bitcast.13, bf16[64,128]{1,0:T(8,128)(2,1)} %bitcast.16, bf16[64,2048]{1,0:T(8,128)(2,1)} %bitcast.14), custom_call_target="tpu_custom_call" | custom-call | flops 1946157056 | bytes 4194304 | tf_op jit(solution)/shard_map/pallas_call | solution.py:428
  42.6 2.3 %copy.9 = bf16[1,1,512,1024]{3,2,1,0:T(8,128)(2,1)} copy(bf16[1,1,512,1024]{3,2,1,0:T(8,128)(2,1)} %bitcast.10) | data formatting | bytes 2097152
